TPU v7x, 512 devices: a whole 4x8x8 slice. The times are simulated.
512 devices in a mesh: chan: 32 (over z_lo, x, core), seg: 16 (over y, z_hi).
Axes of the slice: x: 4, y: 8, z: 8 (z_hi: 2, z_lo: 4; z = z_hi * 4 + z_lo), core: 2. Of those that a mesh axis runs over, the one named last changes fastest.
Arguments:
- strain: float32 [2048, 16, 2048], P('chan', 'seg'), may hold values from -200 to 200
- validity: int32 [2048, 16], P('chan', 'seg'), may hold values from 0 to 1, as said below
- plan: int32 [2], replicated, may hold values from 1 to 3, as said below
Outputs:
- correlations: float32 [2, 2048, 64, 401], P(None, ('chan', 'seg'))
Inputs may be any that keep to these rules, and one draw needn't show every extreme that they name: `plan`: distinct pairing offsets. `validity`: some channels are unusable in every segment.
All inputs are finite; a program needn't handle non-finite values.
Results may differ from a plain program's by a relative error of at most 0.0044.
Values may be sent and summed in bfloat16 or wider, within the bound.
A program may use at most 64 MiB of HBM per device.

v0:
```python
import math

import jax
import jax.numpy as jnp
from jax import lax
from jax.sharding import PartitionSpec as P

SMOOTH = 32
HALF_LAGS = 200
ROUNDS = 2
REACH_BITS = 2


EPSILON = 1e-05


def from_behind(x, axis, by):
    count = lax.axis_size(axis)
    return lax.ppermute(x, axis, [(i, (i + by) % count) for i in range(count)])


def forward_table(first_bin, bin_count, samples):
    sample_index = jnp.arange(samples, dtype=jnp.int32)
    bin_index = first_bin + 1 + jnp.arange(bin_count, dtype=jnp.int32)
    angles = jnp.mod(sample_index[:, None] * bin_index[None, :], samples).astype(jnp.float32) * (
        2.0 * math.pi / samples
    )
    return jnp.concatenate([jnp.cos(angles), -jnp.sin(angles)], axis=1)


def lag_table(first_bin, bin_count, samples, total_bins):
    bin_index = first_bin + 1 + jnp.arange(bin_count, dtype=jnp.int32)
    lag_index = jnp.arange(-HALF_LAGS, HALF_LAGS + 1, dtype=jnp.int32)
    angles = jnp.mod(bin_index[:, None] * lag_index[None, :], samples).astype(jnp.float32) * (
        2.0 * math.pi / samples
    )
    weight = 2.0 / math.sqrt(total_bins)
    return jnp.concatenate([weight * jnp.cos(angles), -weight * jnp.sin(angles)], axis=0)


def spectra(records):
    samples = records.shape[1]
    total_bins = samples // 2
    block_bins = min(128, total_bins)
    count_rows = records.shape[0]

    def one_block(block_number):
        table = forward_table(block_number * block_bins, block_bins, samples)
        return jnp.dot(
            records, table, precision=lax.Precision.HIGHEST, preferred_element_type=jnp.float32
        )

    blocks = lax.map(one_block, jnp.arange(total_bins // block_bins, dtype=jnp.int32))
    blocks = blocks.reshape(total_bins // block_bins, count_rows, 2, block_bins)
    return jnp.transpose(blocks, (1, 2, 0, 3)).reshape(count_rows, 2, total_bins)


def whiten(spectrum, weights):
    magnitude = jnp.sqrt(spectrum[:, 0] * spectrum[:, 0] + spectrum[:, 1] * spectrum[:, 1])
    window = 2 * SMOOTH + 1
    summed = lax.reduce_window(
        magnitude,
        jnp.zeros((), magnitude.dtype),
        lax.add,
        (1, window),
        (1, 1),
        ((0, 0), (SMOOTH, SMOOTH)),
    )
    smoothed = summed / window
    factor = weights[:, None] / (smoothed + EPSILON)
    return (spectrum * factor[:, None, :]).astype(jnp.bfloat16)


def cross_spectral(own_block, partner_block):
    real_real = jnp.einsum(
        "isk,jsk->ijk",
        own_block[:, :, 0],
        partner_block[:, :, 0],
        preferred_element_type=jnp.float32,
    )
    imag_imag = jnp.einsum(
        "isk,jsk->ijk",
        own_block[:, :, 1],
        partner_block[:, :, 1],
        preferred_element_type=jnp.float32,
    )
    imag_real = jnp.einsum(
        "isk,jsk->ijk",
        own_block[:, :, 1],
        partner_block[:, :, 0],
        preferred_element_type=jnp.float32,
    )
    real_imag = jnp.einsum(
        "isk,jsk->ijk",
        own_block[:, :, 0],
        partner_block[:, :, 1],
        preferred_element_type=jnp.float32,
    )
    return jnp.stack([real_real + imag_imag, imag_real - real_imag], axis=2)


def fetch_partner(data, masks, offsets):
    rounds_here = offsets.shape[0]
    for bit_number in range(REACH_BITS):
        arrived_data, arrived_masks = from_behind((data, masks), "chan", 1 << bit_number)
        chosen = offsets // (1 << bit_number) % 2 == 1
        data = jnp.where(
            chosen.reshape((rounds_here,) + (1,) * (data.ndim - 1)), arrived_data, data
        )
        masks = jnp.where(
            chosen.reshape((rounds_here,) + (1,) * (masks.ndim - 1)), arrived_masks, masks
        )
    return (data, masks)


def shards(strain, validity, plan):
    own_rows, seg_dev, samples = strain.shape
    total_bins = samples // 2
    seg_count = lax.axis_size("seg")
    out_rows = own_rows // seg_count
    out_start = lax.axis_index("seg") * out_rows
    spectrum = spectra(strain.reshape(own_rows * seg_dev, samples))
    weights = validity.astype(jnp.float32).reshape(-1)
    whitened = whiten(spectrum, weights).reshape(own_rows, seg_dev, 2, total_bins)
    every_mask = lax.all_gather(validity, "seg", axis=1, tiled=True).astype(jnp.bfloat16)
    own_mask = lax.dynamic_slice_in_dim(every_mask, out_start, out_rows, 0)
    arranged = lax.all_to_all(whitened, "seg", split_axis=3, concat_axis=1, tiled=True)
    lag_weights = lag_table(0, total_bins, samples, total_bins)
    stacked_list = []
    count_list = []
    for round_number in range(ROUNDS):
        partners, partner_masks = fetch_partner(
            arranged[None], every_mask[None], plan[round_number : round_number + 1]
        )
        spectral = cross_spectral(arranged, partners[0])
        to_spectral = lax.all_to_all(spectral, "seg", split_axis=0, concat_axis=3, tiled=True)
        leading = to_spectral.shape[:-2]
        flat = to_spectral.reshape(-1, to_spectral.shape[-2] * to_spectral.shape[-1])
        lagged = jnp.dot(
            flat, lag_weights, precision=lax.Precision.HIGHEST, preferred_element_type=jnp.float32
        )
        stacked_list.append(lagged.reshape(leading + (lag_weights.shape[1],)))
        count_list.append(
            jnp.einsum("is,rjs->rij", own_mask, partner_masks, preferred_element_type=jnp.float32)
        )
    stacked = jnp.stack(stacked_list, axis=0)
    counts = jnp.concatenate(count_list, axis=0)
    return stacked / jnp.maximum(counts, 1.0)[..., None]


def solution(mesh):
    placed = (P("chan", "seg", None), P("chan", "seg"), P())
    return jax.shard_map(
        shards,
        mesh=mesh,
        in_specs=placed,
        out_specs=P(None, ("chan", "seg"), None, None),
        check_vma=False,
    )
```

profile of v0, /device:TPU:1, one launch (start us, length us, event | category | flops | bytes accessed | tf_op | source)
XLA Modules:
  0.0 422.0 jit_solution(17123174309893574861)
XLA Ops:
  1.2 54.5 %while.12 = (s32[]{:T(128)}, f32[8,64,256]{2,1,0:T(8,128)S(1)}, s32[8]{0:T(128)S(1)}, f32[64,2048]{1,0:T(8,128)S(1)}, s32[]{:T(128)}, /*index=5*/s32[1]{0:T(128)}, s32[1]{0:T(128)}) while((s32[]{:T(128)}, f32[8,64,256]{2,1,0:T(8,128)S(1)}, s32[8]{0:T(128)S(1)}, f32[64,2048]{1,0:T(8,128)S(1)}, s32[]{:T(128)}, /*index=5*/s32[1]{0:T(128)}, ...), condition=%wide.region_1.2_spmd, body=%wide.region_0.1_spmd.sunk | while | flops 407109760 | bytes 4785281 | solution.py:53
  2.5 4.1 fusion.56
  9.3 4.1 fusion.56
  16.1 4.1 fusion.56
  22.9 4.1 fusion.56
  29.6 4.1 fusion.56
  36.4 4.1 fusion.56
  56.6 8.8 %reduce_window.10 = f32[64,1024]{1,0:T(8,128)S(1)} reduce-window(f32[64,1024]{1,0:T(8,128)S(1)} %fusion.27, f32[]{:T(128)} %constant.168.clone.1), window={size=1x65 pad=0_0x32_32}, to_apply=%region_2.3 | reduce-window | flops 4194304 | bytes 524292 | tf_op jit(solution)/shard_map/reduce_window | solution.py:61
  66.4 30.4 %all_to_all.48 = bf16[16,2,4096]{2,1,0:T(2,128)(2,1)S(1)} all-to-all(bf16[16,2,4096]{2,1,0:T(2,128)(2,1)S(1)} %reshape.170), channel_id=1, replica_groups=mesh['chan'=32,'seg'=16] {'seg'}, dimensions={0} | all-to-all | bytes 524288 | tf_op jit(solution)/shard_map/all_to_all | solution.py:127
  97.5 6.0 %collective-permute-start = (bf16[1,64,16,2,64]{1,2,4,3,0:T(8,128)(2,1)S(1)}, bf16[1,64,16,2,64]{1,2,4,3,0:T(8,128)(2,1)S(1)}, u32[]{:S(2)}, u32[]{:S(2)}) collective-permute-start(bf16[1,64,16,2,64]{1,2,4,3,0:T(8,128)(2,1)S(1)} %bitcast.163), channel_id=1, source_target_pairs={{0,16},{16,32},{32,48},{48,64},{64,80},{80,96},{96,112},{112,128},... | collective-permute-start | bytes 786440 | tf_op jit(solution)/shard_map/ppermute | solution.py:19
  113.5 10.1 %collective-permute-done.2 = bf16[1,64,16,2,64]{1,2,4,3,0:T(8,128)(2,1)S(1)} collective-permute-done((bf16[1,64,16,2,64]{1,2,4,3,0:T(8,128)(2,1)S(1)}, bf16[1,64,16,2,64]{1,2,4,3,0:T(8,128)(2,1)S(1)}, u32[]{:S(2)}, u32[]{:S(2)}) %collective-permute-start.2) | collective-permute-done | bytes 262176 | tf_op jit(solution)/shard_map/ppermute | solution.py:19
  128.0 5.7 %copy.22 = f32[64,64,2,64]{1,3,2,0:T(8,128)} copy(f32[64,64,2,64]{0,1,3,2:T(8,128)} %pad_maximum_fusion.1) | data formatting | bytes 4194304 | tf_op jit(solution)/shard_map/stack | solution.py:99
  133.7 5.5 %reshape.172 = f32[16,1,32768]{2,1,0:T(1,128)} reshape(f32[64,2,64,64]{3,2,1,0:T(8,128)} %bitcast.159) | data formatting | bytes 4194304
  145.5 19.4 %collective-permute-done.1 = bf16[1,64,16,2,64]{1,2,4,3,0:T(8,128)(2,1)S(1)} collective-permute-done((bf16[1,64,16,2,64]{1,2,4,3,0:T(8,128)(2,1)S(1)}, bf16[1,64,16,2,64]{1,2,4,3,0:T(8,128)(2,1)S(1)}, u32[]{:S(2)}, u32[]{:S(2)}) %collective-permute-start.1) | collective-permute-done | bytes 262176 | tf_op jit(solution)/shard_map/ppermute | solution.py:19
  169.4 5.7 %copy.19 = f32[64,64,2,64]{1,3,2,0:T(8,128)} copy(f32[64,64,2,64]{0,1,3,2:T(8,128)} %pad_maximum_fusion) | data formatting | bytes 4194304 | tf_op jit(solution)/shard_map/stack | solution.py:99
  175.1 5.5 %reshape.174 = f32[16,1,32768]{2,1,0:T(1,128)} reshape(f32[64,2,64,64]{3,2,1,0:T(8,128)} %bitcast.160) | data formatting | bytes 4194304
  180.6 13.4 %all-to-all-done.2 = f32[16,1,32768]{2,1,0:T(1,128)S(1)} async-done(((f32[16,1,32768]{2,1,0:T(1,128)}), f32[16,1,32768]{2,1,0:T(1,128)S(1)}, u32[]{:S(2)}, u32[]{:S(2)}) %all-to-all-start.2) | async-done | bytes 2097184 | tf_op jit(solution)/shard_map/all_to_all | solution.py:136
  195.4 21.7 %all-to-all-start.1 = ((f32[16,1,32768]{2,1,0:T(1,128)}), f32[16,1,32768]{2,1,0:T(1,128)}, u32[]{:S(2)}, u32[]{:S(2)}) async-start(f32[16,1,32768]{2,1,0:T(1,128)} %reshape.174), calls=%async_computation.1 | async-start | bytes 4194304 | tf_op jit(solution)/shard_map/all_to_all | solution.py:136
  217.1 98.5 %all-gather = s32[16,1,64]{2,1,0:T(1,128)S(1)} all-gather(s32[1,1,64]{2,1,0:T(1,128)S(1)} %bitcast.180), channel_id=1, replica_groups=mesh['chan'=32,'seg'=16] {'seg'}, dimensions={0}, use_global_device_ids=true | all-gather | bytes 4352 | tf_op jit(solution)/shard_map/all_gather | solution.py:125
  315.6 10.8 %collective-permute-start.3 = (bf16[1,64,16]{1,2,0:T(8,128)(2,1)S(1)}, bf16[1,64,16]{1,2,0:T(8,128)(2,1)S(1)}, u32[]{:S(2)}, u32[]{:S(2)}) collective-permute-start(bf16[1,64,16]{1,2,0:T(8,128)(2,1)S(1)} %convert_bitcast_fusion.1), channel_id=1, source_target_pairs={{0,16},{16,32},{32,48},{48,64},{64,80},{80,96},{96,112},{112,128},... | collective-permute-start | bytes 6152 | tf_op jit(solution)/shard_map/ppermute | solution.py:19
  327.2 19.9 %collective-permute-start.4 = (bf16[1,64,16]{1,2,0:T(8,128)(2,1)S(1)}, bf16[1,64,16]{1,2,0:T(8,128)(2,1)S(1)}, u32[]{:S(2)}, u32[]{:S(2)}) collective-permute-start(bf16[1,64,16]{1,2,0:T(8,128)(2,1)S(1)} %get-tuple-element.74), channel_id=1, source_target_pairs={{0,32},{16,48},{32,64},{48,80},{64,96},{80,112},{96,128},{112,144}... | collective-permute-start | bytes 6152 | tf_op jit(solution)/shard_map/ppermute | solution.py:19
  347.1 6.7 %cosine_multiply_fusion = (f32[1024,401]{0,1:T(8,128)S(1)}, f32[1024,401]{0,1:T(8,128)S(1)}) fusion(s32[401]{0:T(512)S(1)} %iota_add_fusion.2, s32[1024]{0:T(1024)S(1)} %iota_add_fusion.1), kind=kLoop, calls=%fused_computation.37 | loop fusion | flops 6569984 | bytes 3290692 | tf_op jit(solution)/shard_map/mul | solution.py:38
  353.8 5.3 %collective-permute-start.5 = (bf16[1,64,16]{1,2,0:T(8,128)(2,1)S(1)}, bf16[1,64,16]{1,2,0:T(8,128)(2,1)S(1)}, u32[]{:S(2)}, u32[]{:S(2)}) collective-permute-start(bf16[1,64,16]{1,2,0:T(8,128)(2,1)S(1)} %get-tuple-element.75), channel_id=1, source_target_pairs={{0,32},{16,48},{32,64},{48,80},{64,96},{80,112},{96,128},{112,144}... | collective-permute-start | bytes 6152 | tf_op jit(solution)/shard_map/ppermute | solution.py:19
  362.8 8.7 %reduce = f32[16,32768]{1,0:T(8,128)} reduce(f32[16,1,32768]{2,1,0:T(1,128)} %copy-done.1, f32[]{:T(128)} %broadcast.109), dimensions={1}, to_apply=%all_to_all.42.reduce_sub_computation | reduce | bytes 4194308 | tf_op jit(solution)/shard_map/all_to_all | solution.py:136
  371.5 4.4 %reshape.173 = f32[64,2,64,64]{3,2,1,0:T(8,128)} reshape(f32[16,32768]{1,0:T(8,128)} %reduce) | data formatting | bytes 4194304
  375.9 6.3 %copy.24 = f32[4,64,2,16,64]{4,3,2,1,0:T(8,128)} copy(f32[4,64,2,16,64]{1,4,2,0,3:T(8,128)} %bitcast.161) | data formatting | bytes 4194304 | tf_op jit(solution)/shard_map/all_to_all | solution.py:136
  382.2 5.0 %reshape.160 = f32[4,64,2048]{2,1,0:T(8,128)} reshape(f32[4,64,2,16,64]{4,3,2,1,0:T(8,128)} %copy.24) | data formatting | bytes 4194304 | tf_op jit(solution)/shard_map/reshape.56
  387.2 8.6 %reduce.1 = f32[16,32768]{1,0:T(8,128)} reduce(f32[16,1,32768]{2,1,0:T(1,128)} %all-to-all-done.1, f32[]{:T(128)} %broadcast.109), dimensions={1}, to_apply=%all_to_all.39.reduce_sub_computation | reduce | bytes 4194308 | tf_op jit(solution)/shard_map/all_to_all | solution.py:136
  395.8 4.2 %reshape.175 = f32[64,2,64,64]{3,2,1,0:T(8,128)} reshape(f32[16,32768]{1,0:T(8,128)} %reduce.1) | data formatting | bytes 4194304
  400.0 6.2 %copy.21 = f32[4,64,2,16,64]{4,3,2,1,0:T(8,128)} copy(f32[4,64,2,16,64]{1,4,2,0,3:T(8,128)} %bitcast.162) | data formatting | bytes 4194304 | tf_op jit(solution)/shard_map/all_to_all | solution.py:136
  406.3 5.2 %reshape.159 = f32[4,64,2048]{2,1,0:T(8,128)} reshape(f32[4,64,2,16,64]{4,3,2,1,0:T(8,128)} %copy.21) | data formatting | bytes 4194304 | tf_op jit(solution)/shard_map/reshape.49
  411.5 5.3 %fusion.24 = f32[1,4,64,401]{3,2,1,0:T(8,128)S(1)} fusion(f32[4,64,2048]{2,1,0:T(8,128)} %reshape.160, f32[1024,401]{0,1:T(8,128)S(1)} %get-tuple-element.77, f32[1024,401]{0,1:T(8,128)S(1)} %get-tuple-element.76), kind=kOutput, calls=%fused_computation.39 | convolution fusion | flops 2523695104 | bytes 5792768 | tf_op jit(solution)/shard_map/dot_general | solution.py:139
  (82 shorter events, 58.7 us)
Async XLA Ops:
  55.7 0.8 copy-start.3
  65.6 37.9 %copy-start.2 = (s32[2]{0:T(128)S(1)}, s32[2]{0:T(128)}, u32[]{:S(2)}) copy-start(s32[2]{0:T(128)} %param.7) | copy-start | bytes 28
  97.5 11.7 %collective-permute-start = (bf16[1,64,16,2,64]{1,2,4,3,0:T(8,128)(2,1)S(1)}, bf16[1,64,16,2,64]{1,2,4,3,0:T(8,128)(2,1)S(1)}, u32[]{:S(2)}, u32[]{:S(2)}) collective-permute-start(bf16[1,64,16,2,64]{1,2,4,3,0:T(8,128)(2,1)S(1)} %bitcast.163), channel_id=1, source_target_pairs={{0,16},{16,32},{32,48},{48,64},{64,80},{80,96},{96,112},{112,128},... | collective-permute-start | bytes 786440 | tf_op jit(solution)/shard_map/ppermute | solution.py:19
  109.8 13.8 %collective-permute-start.2 = (bf16[1,64,16,2,64]{1,2,4,3,0:T(8,128)(2,1)S(1)}, bf16[1,64,16,2,64]{1,2,4,3,0:T(8,128)(2,1)S(1)}, u32[]{:S(2)}, u32[]{:S(2)}) collective-permute-start(bf16[1,64,16,2,64]{1,2,4,3,0:T(8,128)(2,1)S(1)} %get-tuple-element.71), channel_id=1, source_target_pairs={{0,32},{16,48},{32,64},{48,80},{64,96},{80,112},{96,128},{112,144}... | collective-permute-start | bytes 786440 | tf_op jit(solution)/shard_map/ppermute | solution.py:19
  139.2 54.8 %all-to-all-start.2 = ((f32[16,1,32768]{2,1,0:T(1,128)}), f32[16,1,32768]{2,1,0:T(1,128)S(1)}, u32[]{:S(2)}, u32[]{:S(2)}) async-start(f32[16,1,32768]{2,1,0:T(1,128)} %reshape.172), calls=%async_computation.2 | async-start | bytes 4194304 | tf_op jit(solution)/shard_map/all_to_all | solution.py:136
  142.9 22.0 %collective-permute-start.1 = (bf16[1,64,16,2,64]{1,2,4,3,0:T(8,128)(2,1)S(1)}, bf16[1,64,16,2,64]{1,2,4,3,0:T(8,128)(2,1)S(1)}, u32[]{:S(2)}, u32[]{:S(2)}) collective-permute-start(bf16[1,64,16,2,64]{1,2,4,3,0:T(8,128)(2,1)S(1)} %get-tuple-element.70), channel_id=1, source_target_pairs={{0,32},{16,48},{32,64},{48,80},{64,96},{80,112},{96,128},{112,144}... | collective-permute-start | bytes 786440 | tf_op jit(solution)/shard_map/ppermute | solution.py:19
  194.0 1.3 copy-start.1
  195.4 191.8 %all-to-all-start.1 = ((f32[16,1,32768]{2,1,0:T(1,128)}), f32[16,1,32768]{2,1,0:T(1,128)}, u32[]{:S(2)}, u32[]{:S(2)}) async-start(f32[16,1,32768]{2,1,0:T(1,128)} %reshape.174), calls=%async_computation.1 | async-start | bytes 4194304 | tf_op jit(solution)/shard_map/all_to_all | solution.py:136
  315.6 11.6 %collective-permute-start.3 = (bf16[1,64,16]{1,2,0:T(8,128)(2,1)S(1)}, bf16[1,64,16]{1,2,0:T(8,128)(2,1)S(1)}, u32[]{:S(2)}, u32[]{:S(2)}) collective-permute-start(bf16[1,64,16]{1,2,0:T(8,128)(2,1)S(1)} %convert_bitcast_fusion.1), channel_id=1, source_target_pairs={{0,16},{16,32},{32,48},{48,64},{64,80},{80,96},{96,112},{112,128},... | collective-permute-start | bytes 6152 | tf_op jit(solution)/shard_map/ppermute | solution.py:19
  327.2 31.9 %collective-permute-start.4 = (bf16[1,64,16]{1,2,0:T(8,128)(2,1)S(1)}, bf16[1,64,16]{1,2,0:T(8,128)(2,1)S(1)}, u32[]{:S(2)}, u32[]{:S(2)}) collective-permute-start(bf16[1,64,16]{1,2,0:T(8,128)(2,1)S(1)} %get-tuple-element.74), channel_id=1, source_target_pairs={{0,32},{16,48},{32,64},{48,80},{64,96},{80,112},{96,128},{112,144}... | collective-permute-start | bytes 6152 | tf_op jit(solution)/shard_map/ppermute | solution.py:19
  353.8 8.3 %collective-permute-start.5 = (bf16[1,64,16]{1,2,0:T(8,128)(2,1)S(1)}, bf16[1,64,16]{1,2,0:T(8,128)(2,1)S(1)}, u32[]{:S(2)}, u32[]{:S(2)}) collective-permute-start(bf16[1,64,16]{1,2,0:T(8,128)(2,1)S(1)} %get-tuple-element.75), channel_id=1, source_target_pairs={{0,32},{16,48},{32,64},{48,80},{64,96},{80,112},{96,128},{112,144}... | collective-permute-start | bytes 6152 | tf_op jit(solution)/shard_map/ppermute | solution.py:19
  411.4 5.4 %copy-start = (f32[4,64,2048]{2,1,0:T(8,128)S(1)}, f32[4,64,2048]{2,1,0:T(8,128)}, u32[]{:S(2)}) copy-start(f32[4,64,2048]{2,1,0:T(8,128)} %reshape.159) | copy-start | bytes 6291460
where the time goes:
time: 428 us; the launch traced here: 422 us
  blocking collectives  129 us (30%)
  other arithmetic  72.8 us (17%)
  starting transfers between devices  72.5 us (17%)
  local copies, waits for them, and re-layouts  64.7 us (15%)
  waiting for transfers between devices  47.9 us (11%)
  matrix products  24.1 us (6%)
  between operations  5.73 us (1%)
  loops' own time  5.42 us (1%)
    all_gather x1, blocking collectives, shards(): lax.all_gather(validity, 'seg', axis=1, tiled=True).astype(jnp.bfloat16)  98.5 us
    ppermute x6, starting transfers between devices, from_behind(): return lax.ppermute(x, axis, [(i, (i + by) % count) for i in range(count)])  47 us
    ppermute x6, waiting for transfers between devices, from_behind(): return lax.ppermute(x, axis, [(i, (i + by) % count) for i in range(count)])  34.4 us
    cos x8, other arithmetic, forward_table(): return jnp.concatenate([jnp.cos(angles), -jnp.sin(angles)], axis=1)  33.1 us
    all_to_all x1, blocking collectives, shards(): lax.all_to_all(whitened, 'seg', split_axis=3, concat_axis=1, tiled=True)  30.4 us
    all_to_all x2, starting transfers between devices, shards(): lax.all_to_all(spectral, 'seg', split_axis=0, concat_axis=3, tiled=True)  25.5 us
    unnamed x15, local copies, waits for them, and re-layouts  23 us
    all_to_all x2, other arithmetic, shards(): lax.all_to_all(spectral, 'seg', split_axis=0, concat_axis=3, tiled=True)  17.3 us
  transfers between devices with their start and end apart: 8, of which 6 were waited for; matrix products, arithmetic and copies ran while one was open for 11% of the time, Pallas kernels for 0%

commit v1 on v0

v1 whole, which is shorter than its diff:
```python
import math

import jax
import jax.numpy as jnp
import ml_dtypes
import numpy as np
from jax import lax
from jax.experimental import pallas as pl
from jax.experimental.pallas import tpu as pltpu
from jax.sharding import PartitionSpec as P

MESH = pl.DeviceIdType.MESH
SMOOTH = 32
HALF_LAGS = 200
LAGS = 2 * HALF_LAGS + 1
SAMPLES = 2048
BINS = 1024
EPSILON = 1e-05
ROUNDS = 2
F32 = jnp.float32
BF16 = jnp.bfloat16


def place(r):
    if r == 8 or r == 16:
        return 0, r // 16
    return (r, 0) if r < 8 else (16 - r, 1)


def split(table):
    high = table.astype(ml_dtypes.bfloat16)
    low = (table - high.astype(np.float64)).astype(ml_dtypes.bfloat16)
    return high, low


def dft_tables():
    c = np.arange(128)[:, None]
    q = np.arange(64)[None, :]

    def angle(steps, period):
        return 2.0 * np.pi * np.mod(steps, period) / period

    low, high = angle(c * q, 128), angle(c * (127 - q), 128)
    first = np.zeros((256, 256))
    first[:128, 0:64], first[128:, 0:64] = np.cos(low), np.sin(low)
    first[:128, 64:128], first[128:, 64:128] = -np.sin(low), np.cos(low)
    first[:128, 128:192], first[128:, 128:192] = np.cos(high), np.sin(high)
    first[:128, 192:256], first[128:, 192:256] = np.sin(high), -np.cos(high)
    eight, sixteen = angle(c * (8 + 16 * q), SAMPLES), angle(c * (16 + 16 * q), SAMPLES)
    second = np.zeros((256, 256))
    second[128:, 0:64], second[128:, 64:128] = np.cos(eight), -np.sin(eight)
    second[:128, 128:192], second[:128, 192:256] = np.cos(sixteen), -np.sin(sixteen)
    turn = angle(np.arange(8)[:, None] * np.arange(128)[None, :], SAMPLES)
    twiddle = np.concatenate([np.cos(turn), np.sin(turn)], axis=0).astype(np.float32)
    return split(first) + split(second) + (twiddle,)


def lag_table():
    lag = np.arange(-HALF_LAGS, HALF_LAGS + 1)[None, :]
    weight = 2.0 / math.sqrt(BINS)
    table = np.zeros((8, 256, 512))
    for r in range(1, 17):
        slab, half = place(r)
        turn = 2.0 * np.pi * np.mod((r + 16 * np.arange(64)[:, None]) * lag, SAMPLES) / SAMPLES
        table[slab, 128 * half : 128 * half + 64, :LAGS] = weight * np.cos(turn)
        table[slab, 128 * half + 64 : 128 * half + 128, :LAGS] = -weight * np.sin(turn)
    return table.astype(ml_dtypes.bfloat16)


def first_stage(x):
    root = math.sqrt(0.5)
    e = [x[a] + x[a + 8] for a in range(8)]
    o = [x[a] - x[a + 8] for a in range(8)]
    ee = [e[a] + e[a + 4] for a in range(4)]
    eo = [e[a] - e[a + 4] for a in range(4)]
    y = {}
    even, odd = ee[0] + ee[2], ee[1] + ee[3]
    y[0], y[8] = even + odd, even - odd
    y[4] = (ee[0] - ee[2], ee[3] - ee[1])
    minus, plus = root * (eo[1] - eo[3]), root * (eo[1] + eo[3])
    y[2] = (eo[0] + minus, -(eo[2] + plus))
    y[6] = (eo[0] - minus, eo[2] - plus)
    dm = [None] + [o[a] - o[8 - a] for a in (1, 2, 3)]
    dp = [None] + [o[a] + o[8 - a] for a in (1, 2, 3)]
    for k in (1, 3, 5, 7):
        real, imag = o[0], o[4] * math.sin(math.pi * k / 2)
        for a in (1, 2, 3):
            real = real + math.cos(2 * math.pi * a * k / 16) * dm[a]
            imag = imag + math.sin(2 * math.pi * a * k / 16) * dp[a]
        y[k] = (real, -imag)
    return y


def kernel(
    plan, x, valid, t1h, t1l, t2h, t2l, twiddle, lag_hbm, out,
    zh_, zl_, spec, ws, zw, wg, v, fl, fv, fpad, fto, ctab, crecv, inv,
    a_, b_, c_, d_, xs, xr, lag, keep, zs, zr,
    lag_sem, y1s, y1r, zws, zwr, y2s, y2r, p_s, p_r, f1s, f1r, fxs, fxr, cs, cr, ys, yr, zss, zrr,
):
    chan, seg = lax.axis_index("chan"), lax.axis_index("seg")
    core = lax.rem(chan, 2)
    y, zh = seg // 2, lax.rem(seg, 2)
    oz = 1 - zh
    kappa = lax.rem(y, 4)

    def at_y(step):
        return lax.rem(y + step, 8)

    def chan_at(step):
        return lax.rem(chan + step + 32, 32)

    def on_y(row):
        return (chan, 2 * row + zh)

    other = (chan, 2 * y + oz)
    ahead = (chan_at(2), seg)
    jump = (chan_at(1 + 2 * core), seg)
    mate = (chan_at(1 - 2 * core), seg)

    def remote(src, dst, send, recv, device):
        return pltpu.make_async_remote_copy(
            src_ref=src, dst_ref=dst, send_sem=send, recv_sem=recv, device_id=device, device_id_type=MESH
        )

    barrier = pltpu.get_barrier_semaphore()
    senders = [on_y(at_y(s)) for s in range(1, 8)] + [other]
    senders += [(chan_at(-2), seg), (chan_at(-3 + 2 * core), seg), mate]
    for device in senders:
        pl.semaphore_signal(barrier, inc=1, device_id=device, device_id_type=MESH)
    lag_copy = pltpu.make_async_copy(lag_hbm.at[pl.ds(4 * zh, 4)], lag, lag_sem)
    lag_copy.start()

    def transform(g, carry):
        rows = pl.ds(pl.multiple_of(g * 16, 16), 16)
        ys_ = first_stage([x[rows, 128 * s : 128 * s + 128] for s in range(16)])
        pairs = [(ys_[0], ys_[8])]
        for k in range(1, 8):
            real, imag = ys_[k]
            co, si = twiddle[k : k + 1, :], twiddle[8 + k : 9 + k, :]
            pairs.append((real * co + imag * si, imag * co - real * si))
        for j in range(8):
            for part in range(2):
                high = pairs[j][part].astype(BF16)
                zh_[j, rows, 128 * part : 128 * part + 128] = high
                zl_[j, rows, 128 * part : 128 * part + 128] = (pairs[j][part] - high.astype(F32)).astype(BF16)
        return carry

    lax.fori_loop(0, 4, transform, 0)

    def product(high, low, th, tl):
        total = jnp.dot(high, tl[...], preferred_element_type=F32)
        total += jnp.dot(low, th[...], preferred_element_type=F32)
        return total + jnp.dot(high, th[...], preferred_element_type=F32)

    spec[0] = product(zh_[0], zl_[0], t2h, t2l)
    main = product(zh_[1:8].reshape(448, 256), zl_[1:8].reshape(448, 256), t1h, t1l)
    spec[1:8] = main.reshape(7, 64, 256)

    lane = lax.broadcasted_iota(jnp.int32, (16, 128), 1)
    q = jnp.bitwise_and(lane, 63)

    def shifted(value, by):
        moved = pltpu.roll(value, (128 - by) % 128, 1)
        kept = q < 64 - by if by > 0 else q >= -by
        return jnp.where(kept, moved, 0.0)

    def whiten(g, carry):
        rows = pl.ds(pl.multiple_of(g * 16, 16), 16)
        mags = []
        for r in range(1, 17):
            slab, half = place(r)
            value = spec[slab, rows, 128 * half : 128 * half + 128]
            square = value * value
            mags.append(jnp.sqrt(square + pltpu.roll(square, 64, 1)))
        below, above = [mags[0]], [mags[15]]
        for r in range(1, 16):
            below.append(below[-1] + mags[r])
            above.append(above[-1] + mags[15 - r])
        above = above[::-1]
        whole = below[15]
        middle = shifted(whole, -1) + whole + shifted(whole, 1)
        weight = valid[rows, :].astype(F32)
        for r in range(1, 17):
            slab, half = place(r)
            window = shifted(above[r - 1], -2) + middle + shifted(below[r - 1], 2)
            factor = weight / (window * (1.0 / (2 * SMOOTH + 1)) + EPSILON)
            value = spec[slab, rows, 128 * half : 128 * half + 128]
            ws[slab, g, :, 128 * half : 128 * half + 128] = (value * factor).astype(BF16)
        return carry

    lax.fori_loop(0, 4, whiten, 0)
    column = jnp.broadcast_to(valid[...].astype(F32), (64, 128))
    fl[y] = jnp.transpose(jnp.concatenate([column, column], axis=0))[0:1, :]

    pl.semaphore_wait(barrier, 11)

    z_sends, y1_sends, y2_sends, f_sends = [], [], [], []
    for step in range(4):
        k = lax.rem(kappa + step, 4)
        z_sends.append(remote(ws.at[4 * oz + k], zw.at[k], zws.at[k], zwr.at[k], other))
        z_sends[-1].start()
    for step in (4, 3, 5, 2, 6, 1, 7):
        row = at_y(step)
        y1_sends.append(
            remote(ws.at[4 * zh + lax.rem(row, 4)], wg.at[zh, :, y], y1s.at[step], y1r.at[step], on_y(row))
        )
        y1_sends[-1].start()
    for step in range(1, 8):
        f_sends.append(remote(fl.at[y], fl.at[y], f1s.at[step], f1r.at[step], on_y(at_y(step))))
        f_sends[-1].start()
    wg[zh, :, y] = ws[4 * zh + kappa]

    def put_p1(half, j):
        piece = wg.at[half, j]
        first = remote(piece, v.at[1, half, j], p_s.at[0, half, j], p_r.at[1, half, j], ahead)
        second = remote(
            piece, v.at[2 * core, half, j], p_s.at[1, half, j], p_r.at[2 * core, half, j], jump
        )
        return first, second

    def put_p2(half, j):
        return remote(
            v.at[1, half, j], v.at[2 - 2 * core, half, j], p_s.at[2, half, j], p_r.at[2 - 2 * core, half, j], mate
        )

    def arrived(slot, half, j):
        remote(v.at[slot, half, j], v.at[slot, half, j], p_s.at[0, half, j], p_r.at[slot, half, j], ahead).wait_recv()

    for copy in y1_sends:
        copy.wait_recv()

    def start_p1(half):
        def body(j, carry):
            for copy in put_p1(half, j):
                copy.start()
            return carry

        lax.fori_loop(0, 4, body, 0)

    start_p1(zh)
    for step in range(4):
        k = lax.rem(kappa + step, 4)
        z_sends[step].wait_recv()
        for far in (4, 0):
            if step + far == 0:
                wg[oz, :, y] = zw[k]
                continue
            row = at_y(step + far)
            y2_sends.append(
                remote(zw.at[k], wg.at[oz, :, y], y2s.at[step + far], y2r.at[step + far], on_y(row))
            )
            y2_sends[-1].start()

    for copy in f_sends:
        copy.wait_recv()
    flag_sends = [
        remote(fl, fv.at[1], fxs.at[0], fxr.at[1], ahead),
        remote(fl, fv.at[2 * core], fxs.at[1], fxr.at[2 * core], jump),
    ]
    for copy in flag_sends:
        copy.start()

    def start_p2(j, carry):
        arrived(1, zh, j)
        put_p2(zh, j).start()
        return carry

    lax.fori_loop(0, 4, start_p2, 0)
    for copy in y2_sends:
        copy.wait_recv()
    start_p1(oz)

    remote(fv.at[1], fv.at[1], fxs.at[0], fxr.at[1], ahead).wait_recv()
    flag_sends.append(remote(fv.at[1], fv.at[2 - 2 * core], fxs.at[2], fxr.at[2 - 2 * core], mate))
    flag_sends[-1].start()

    first_half = lane < 64
    sign = jnp.where(first_half, 1.0, -1.0).astype(F32)

    def spread(s, carry):
        half, row = s // 8, lax.rem(s, 8)
        for j in range(4):
            value = wg[half, j, row].astype(F32)
            for h in range(2):
                one = value[:, 128 * h : 128 * h + 128]
                swapped = pltpu.roll(one, 64, 1)
                a_[s, h, 16 * j : 16 * j + 16, :] = jnp.where(first_half, one, swapped)
                b_[s, h, 16 * j : 16 * j + 16, :] = jnp.where(first_half, swapped, one)
        return carry

    lax.fori_loop(0, 16, spread, 0)

    def chosen(r, options):
        offset = plan[r]
        return jnp.where(offset == 1, options[0], jnp.where(offset == 2, options[1], options[2]))

    def prepare(r, j):
        def body(s, carry):
            half, row = s // 8, lax.rem(s, 8)
            value = chosen(r, [v[d, half, j, row].astype(F32) for d in range(3)])
            for h in range(2):
                one = value[:, 128 * h : 128 * h + 128]
                c_[s, h] = one * sign
                d_[s, h] = pltpu.roll(one, 64, 1)
            return carry

        lax.fori_loop(0, 16, body, 0)

    hops = [2 + 4 * core, 1, 7, 0]

    def cross(r, j, t, target):
        start = pl.multiple_of(8 * at_y(hops[t]), 8)
        for h in range(2):

            def body(s, totals):
                c, d = c_[s, h], d_[s, h]
                mine = [
                    a_[s, h, pl.ds(start + i, 1), :] * c + b_[s, h, pl.ds(start + i, 1), :] * d
                    for i in range(8)
                ]
                return tuple(total + one for total, one in zip(totals, mine))

            totals = lax.fori_loop(0, 16, body, (jnp.zeros((16, 128), F32),) * 8, unroll=2)
            for i in range(8):
                target[16 * i : 16 * i + 16, 128 * h : 128 * h + 128] = totals[i].astype(BF16)

    def put_cross(r, j, t):
        return remote(
            xs.at[r, j, t], xr.at[r, j, kappa], ys.at[r, j, t], yr.at[r, j, t], on_y(at_y(hops[t]))
        )

    def cross_all(r, j):
        prepare(r, j)
        for t in range(3):
            cross(r, j, t, xs.at[r, j, t])
            put_cross(r, j, t).start()
        cross(r, j, 3, xr.at[r, j, kappa])

    def put_lags(r, j):
        return remote(zs.at[r, j], zr.at[r, j], zss.at[r, j], zrr.at[r, j], other)

    def lagged(r, j, side):
        rows = pl.ds(pl.multiple_of(64 * side, 64), 64)
        total = jnp.dot(xr[r, j, 0, rows, :], lag[0], preferred_element_type=F32)
        for k in range(1, 4):
            total += jnp.dot(xr[r, j, k, rows, :], lag[k], preferred_element_type=F32)
        return total

    def lag_stage(r, j):
        for t in range(3):
            put_cross(r, j, t).wait_recv()
        zs[r, j] = lagged(r, j, oz).astype(BF16)
        put_lags(r, j).start()
        keep[r, j] = lagged(r, j, zh)

    def finish(r, j):
        put_lags(r, j).wait_recv()
        total = keep[r, j] + zr[r, j].astype(F32)
        rows = pl.ds(pl.multiple_of(16 * j, 16), 16)
        for i in range(4):
            scale = inv[r, i, rows, 0:1]
            out[r, i, rows, :] = (total[16 * i : 16 * i + 16, :] * scale)[:, :LAGS]

    def start_round(j):
        arrived(1, oz, j)
        put_p2(oz, j).start()

    start_round(0)

    wide = lax.broadcasted_iota(jnp.int32, (64, 128), 1)
    fpad[...] = jnp.zeros((128, 128), F32)
    for s in range(8):
        fpad[s : s + 1, :] = fl[s]
    fto[...] = jnp.transpose(fpad[...])
    remote(fv.at[0], fv.at[0], fxs.at[0], fxr.at[0], ahead).wait_recv()
    remote(fv.at[2], fv.at[2], fxs.at[0], fxr.at[2], ahead).wait_recv()
    table = jnp.zeros((64, 128), F32)
    for r in range(ROUNDS):
        for s in range(8):
            fpad[s : s + 1, :] = chosen(r, [fv[d, s] for d in range(3)])
        partner = jnp.transpose(fpad[...])[0:64, :]
        for i in range(8):
            number = jnp.sum(partner * fto[pl.ds(8 * y + i, 1), :], axis=1, keepdims=True)
            table = jnp.where(wide == 8 * r + i, number, table)
    ctab[...] = table
    count_send = remote(ctab, crecv, cs, cr, other)
    count_send.start()

    lag_copy.wait()

    def main_loop(j, carry):
        arrived(0, zh, j)
        arrived(0, oz, j)
        arrived(2, zh, j)
        arrived(2, oz, j)
        cross_all(0, j)

        @pl.when(j < 3)
        def _():
            start_round(j + 1)

        cross_all(1, j)

        @pl.when(j == 1)
        def _():
            count_send.wait_recv()
            both = ctab[...] + crecv[...]
            for r in range(ROUNDS):
                for i in range(4):
                    number = jnp.sum(
                        jnp.where(wide == 8 * r + 4 * zh + i, both, 0.0), axis=1, keepdims=True
                    )
                    inv[r, i] = jnp.broadcast_to(1.0 / jnp.maximum(number, 1.0), (64, 128))

        @pl.when(j >= 1)
        def _():
            for r in range(ROUNDS):
                lag_stage(r, j - 1)

        @pl.when(j >= 2)
        def _():
            for r in range(ROUNDS):
                finish(r, j - 2)

        return carry

    lax.fori_loop(0, 4, main_loop, 0)
    for r in range(ROUNDS):
        lag_stage(r, 3)
    for j in (2, 3):
        for r in range(ROUNDS):
            finish(r, j)

    for copy in z_sends + y1_sends + y2_sends + f_sends + flag_sends + [count_send]:
        copy.wait_send()

    def drain(j, carry):
        for half in range(2):
            for copy in put_p1(half, j):
                copy.wait_send()
            put_p2(half, j).wait_send()
        for r in range(ROUNDS):
            for t in range(3):
                put_cross(r, j, t).wait_send()
            put_lags(r, j).wait_send()
        return carry

    lax.fori_loop(0, 4, drain, 0)


def shards(strain, validity, plan):
    t1h, t1l, t2h, t2l, twiddle = (jnp.asarray(t) for t in dft_tables())
    lag = jnp.asarray(lag_table())
    vmem = pl.BlockSpec(memory_space=pltpu.VMEM)
    dma = pltpu.SemaphoreType.DMA
    return pl.pallas_call(
        kernel,
        out_shape=jax.ShapeDtypeStruct((ROUNDS, 4, 64, LAGS), F32),
        in_specs=[pl.BlockSpec(memory_space=pltpu.SMEM)] + [vmem] * 7 + [pl.BlockSpec(memory_space=pl.ANY)],
        out_specs=vmem,
        scratch_shapes=[
            pltpu.VMEM((8, 64, 256), BF16),
            pltpu.VMEM((8, 64, 256), BF16),
            pltpu.VMEM((8, 64, 256), F32),
            pltpu.VMEM((8, 4, 16, 256), BF16),
            pltpu.VMEM((4, 4, 16, 256), BF16),
            pltpu.VMEM((2, 4, 8, 16, 256), BF16),
            pltpu.VMEM((3, 2, 4, 8, 16, 256), BF16),
            pltpu.VMEM((8, 1, 128), F32),
            pltpu.VMEM((3, 8, 1, 128), F32),
            pltpu.VMEM((128, 128), F32),
            pltpu.VMEM((128, 128), F32),
            pltpu.VMEM((64, 128), F32),
            pltpu.VMEM((64, 128), F32),
            pltpu.VMEM((2, 4, 64, 128), F32),
            pltpu.VMEM((16, 2, 64, 128), F32),
            pltpu.VMEM((16, 2, 64, 128), F32),
            pltpu.VMEM((16, 2, 16, 128), F32),
            pltpu.VMEM((16, 2, 16, 128), F32),
            pltpu.VMEM((2, 4, 3, 128, 256), BF16),
            pltpu.VMEM((2, 4, 4, 128, 256), BF16),
            pltpu.VMEM((4, 256, 512), BF16),
            pltpu.VMEM((2, 4, 64, 512), F32),
            pltpu.VMEM((2, 4, 64, 512), BF16),
            pltpu.VMEM((2, 4, 64, 512), BF16),
            dma,
            dma((8,)), dma((8,)),
            dma((4,)), dma((4,)),
            dma((8,)), dma((8,)),
            dma((3, 2, 4)), dma((3, 2, 4)),
            dma((8,)), dma((8,)),
            dma((3,)), dma((3,)),
            dma, dma,
            dma((2, 4, 3)), dma((2, 4, 3)),
            dma((2, 4)), dma((2, 4)),
        ],
        compiler_params=pltpu.CompilerParams(
            collective_id=0, has_side_effects=True, vmem_limit_bytes=40 * 1024 * 1024
        ),
        name="correlate",
    )(plan, strain.reshape(64, SAMPLES), validity, t1h, t1l, t2h, t2l, twiddle, lag)


def solution(mesh):
    placed = (P("chan", "seg", None), P("chan", "seg"), P())
    return jax.shard_map(
        shards,
        mesh=mesh,
        in_specs=placed,
        out_specs=P(None, ("chan", "seg"), None, None),
        check_vma=False,
    )
```

time: 428 us -> 93.6 us (0.22); the launches traced: 422 us -> 93.3 us
  blocking collectives: 129 us -> 0 us
  Pallas kernels: 0 us -> 83.8 us
  other arithmetic: 72.8 us -> 0 us
  starting transfers between devices: 72.5 us -> 0 us
  local copies, waits for them, and re-layouts: 64.7 us -> 9.47 us
  waiting for transfers between devices: 47.9 us -> 0 us
  matrix products: 24.1 us -> 0 us
  between operations: 5.73 us -> 0.03 us
  loops' own time: 5.42 us -> 0 us
    all_gather x1 -> x0, blocking collectives: 98.5 us -> none  [shards(): lax.all_gather(validity, 'seg', axis=1, tiled=True).astype(jnp.bfloat16)]
    pallas_call x0 -> x1, Pallas kernels: none -> 83.8 us  [shards(): pl.pallas_call(kernel, out_shape=jax.ShapeDtypeStruct((ROUNDS, 4, 64, LAG...]
    ppermute x6 -> x0, starting transfers between devices: 47 us -> none  [from_behind(): return lax.ppermute(x, axis, [(i, (i + by) % count) for i in range(count)])]
    ppermute x6 -> x0, waiting for transfers between devices: 34.4 us -> none  [from_behind(): return lax.ppermute(x, axis, [(i, (i + by) % count) for i in range(count)])]
    cos x8 -> x0, other arithmetic: 33.1 us -> none  [forward_table(): return jnp.concatenate([jnp.cos(angles), -jnp.sin(angles)], axis=1)]
    all_to_all x1 -> x0, blocking collectives: 30.4 us -> none  [shards(): lax.all_to_all(whitened, 'seg', split_axis=3, concat_axis=1, tiled=True)]
    all_to_all x2 -> x0, starting transfers between devices: 25.5 us -> none  [shards(): lax.all_to_all(spectral, 'seg', split_axis=0, concat_axis=3, tiled=True)]
    dot_general x20 -> x0, matrix products: 24.1 us -> none  [the longest x8 10.7 us: one_block(): jnp.dot(records, table, precision=lax.Precision.HIGHEST, preferred_elemen...]
  transfers between devices with their start and end apart: 8 -> 0, of which waited for: 6 -> 0; matrix products, arithmetic and copies ran while one was open for 11% -> 0% of each run, Pallas kernels for 0% -> 0%
where the time goes in v1:
time: 93.6 us; the launch traced here: 93.3 us
  Pallas kernels  83.8 us (90%)
  local copies, waits for them, and re-layouts  9.47 us (10%)
    pallas_call x1, Pallas kernels, shards(): pl.pallas_call(kernel, out_shape=jax.ShapeDtypeStruct((ROUNDS, 4, 64, LAG...  83.8 us
    unnamed x17, local copies, waits for them, and re-layouts  9.47 us

profile of v1, /device:TPU:1, one launch (start us, length us, event | category | flops | bytes accessed | tf_op | source)
XLA Modules:
  0.0 93.3 jit_solution(7265923367587969805)
XLA Ops:
  0.0 0.7 copy.10.valid
  0.7 1.2 %copy.13 = f32[64,1,2048]{2,0,1:T(8,128)S(1)} copy(f32[64,1,2048]{2,1,0:T(1,128)} %param.9) | data formatting | bytes 1048576
  1.9 0.0 copy-start
  2.0 1.6 %copy-done = bf16[8,256,512]{2,1,0:T(8,128)(2,1)S(1)} copy-done((bf16[8,256,512]{2,1,0:T(8,128)(2,1)S(1)}, bf16[8,256,512]{2,1,0:T(8,128)(2,1)}, u32[]{:S(2)}) %copy-start) | copy-done | bytes 2097176
  3.5 0.0 copy-start.1
  3.5 0.9 copy-done.1
  4.5 0.0 copy-start.2
  4.5 0.9 copy-done.2
  5.4 0.0 copy-start.3
  5.4 0.9 copy-done.3
  6.3 0.0 copy-start.4
  6.3 0.9 copy-done.4
  7.2 0.0 copy-start.5
  7.2 0.7 copy-done.5
  7.9 0.0 copy-start.6
  7.9 0.7 copy-done.6
  8.5 83.8 %correlate.1 = f32[2,4,64,401]{3,2,1,0:T(8,128)S(1)} custom-call(s32[2]{0:T(128)S(1)} %copy-done.6, f32[64,2048]{1,0:T(8,128)S(1)} %bitcast.3, s32[64,1]{1,0:T(8,128)S(1)} %copy.10.valid, bf16[256,256]{1,0:T(8,128)(2,1)S(1)} %copy-done.4, bf16[256,256]{1,0:T(8,128)(2,1)S(1)} %copy-done.3, bf16[256,256]{1,0:T(8,128)(2,1)S(1)} %copy-done.2, ...), custom_call_target="tpu_custom_call" | custom-call | tf_op jit(solution)/shard_map/correlate/pallas_call | solution.py:456
  92.4 1.0 %copy.15 = f32[2,4,64,401]{3,2,1,0:T(8,128)} copy(f32[2,4,64,401]{3,2,1,0:T(8,128)S(1)} %correlate.1) | data formatting | bytes 1642496
Async XLA Ops:
  1.9 1.6 %copy-start = (bf16[8,256,512]{2,1,0:T(8,128)(2,1)S(1)}, bf16[8,256,512]{2,1,0:T(8,128)(2,1)}, u32[]{:S(2)}) copy-start(bf16[8,256,512]{2,1,0:T(8,128)(2,1)} %constant.17.clone.lag_hbm) | copy-start | bytes 6291460
  3.5 0.9 copy-start.1
  4.5 0.9 copy-start.2
  5.4 0.9 copy-start.3
  6.3 0.9 copy-start.4
  7.2 0.7 copy-start.5
  7.9 0.7 copy-start.6

commit v2 on v1

--- a/solution.py
+++ b/solution.py
@@ -92,10 +92,10 @@
 
 
 def kernel(
-    plan, x, valid, t1h, t1l, t2h, t2l, twiddle, lag_hbm, out,
-    zh_, zl_, spec, ws, zw, wg, v, fl, fv, fpad, fto, ctab, crecv, inv,
+    plan_in, x_in, valid_in, t1h_in, t1l_in, t2h_in, t2l_in, twiddle_in, lag_in, out,
+    plan, x, flags, t1h, t1l, t2h, t2l, twiddle, valid, zh_, zl_, spec, ws, zw, wg, v, fl, fv, fpad, fto, ctab, crecv, inv,
     a_, b_, c_, d_, xs, xr, lag, keep, zs, zr,
-    lag_sem, y1s, y1r, zws, zwr, y2s, y2r, p_s, p_r, f1s, f1r, fxs, fxr, cs, cr, ys, yr, zss, zrr,
+    in_sems, y1s, y1r, zws, zwr, y2s, y2r, p_s, p_r, f1s, f1r, fxs, fxr, cs, cr, ys, yr, zss, zrr,
 ):
     chan, seg = lax.axis_index("chan"), lax.axis_index("seg")
     core = lax.rem(chan, 2)
@@ -127,8 +127,17 @@
     senders += [(chan_at(-2), seg), (chan_at(-3 + 2 * core), seg), mate]
     for device in senders:
         pl.semaphore_signal(barrier, inc=1, device_id=device, device_id_type=MESH)
-    lag_copy = pltpu.make_async_copy(lag_hbm.at[pl.ds(4 * zh, 4)], lag, lag_sem)
-    lag_copy.start()
+    loads = [pltpu.make_async_copy(x_in.at[:, 0, :], x, in_sems.at[0])]
+    pairs_in = [(twiddle_in, twiddle), (valid_in, flags), (t1h_in, t1h), (t1l_in, t1l), (t2h_in, t2h), (t2l_in, t2l)]
+    pairs_in += [(plan_in, plan), (lag_in.at[pl.ds(4 * zh, 4)], lag)]
+    for number, (src, dst) in enumerate(pairs_in):
+        loads.append(pltpu.make_async_copy(src, dst, in_sems.at[number + 1]))
+    for copy in loads:
+        copy.start()
+    for copy in loads[:3]:
+        copy.wait()
+    square_flags = jnp.broadcast_to(flags[...].astype(F32), (64, 64))
+    valid[...] = jnp.transpose(square_flags)[:, 0:1]
 
     def transform(g, carry):
         rows = pl.ds(pl.multiple_of(g * 16, 16), 16)
@@ -146,6 +155,9 @@
         return carry
 
     lax.fori_loop(0, 4, transform, 0)
+
+    for copy in loads[3:8]:
+        copy.wait()
 
     def product(high, low, th, tl):
         total = jnp.dot(high, tl[...], preferred_element_type=F32)
@@ -179,7 +191,7 @@
         above = above[::-1]
         whole = below[15]
         middle = shifted(whole, -1) + whole + shifted(whole, 1)
-        weight = valid[rows, :].astype(F32)
+        weight = valid[rows, :]
         for r in range(1, 17):
             slab, half = place(r)
             window = shifted(above[r - 1], -2) + middle + shifted(below[r - 1], 2)
@@ -189,7 +201,7 @@
         return carry
 
     lax.fori_loop(0, 4, whiten, 0)
-    column = jnp.broadcast_to(valid[...].astype(F32), (64, 128))
+    column = jnp.broadcast_to(valid[...], (64, 128))
     fl[y] = jnp.transpose(jnp.concatenate([column, column], axis=0))[0:1, :]
 
     pl.semaphore_wait(barrier, 11)
@@ -288,7 +300,7 @@
                 b_[s, h, 16 * j : 16 * j + 16, :] = jnp.where(first_half, swapped, one)
         return carry
 
-    lax.fori_loop(0, 16, spread, 0)
+    lax.fori_loop(0, 16, spread, 0, unroll=2)
 
     def chosen(r, options):
         offset = plan[r]
@@ -304,7 +316,7 @@
                 d_[s, h] = pltpu.roll(one, 64, 1)
             return carry
 
-        lax.fori_loop(0, 16, body, 0)
+        lax.fori_loop(0, 16, body, 0, unroll=8)
 
     hops = [2 + 4 * core, 1, 7, 0]
 
@@ -386,7 +398,7 @@
     count_send = remote(ctab, crecv, cs, cr, other)
     count_send.start()
 
-    lag_copy.wait()
+    loads[8].wait()
 
     def main_loop(j, carry):
         arrived(0, zh, j)
@@ -456,9 +468,18 @@
     return pl.pallas_call(
         kernel,
         out_shape=jax.ShapeDtypeStruct((ROUNDS, 4, 64, LAGS), F32),
-        in_specs=[pl.BlockSpec(memory_space=pltpu.SMEM)] + [vmem] * 7 + [pl.BlockSpec(memory_space=pl.ANY)],
+        in_specs=[pl.BlockSpec(memory_space=pltpu.HBM)] * 9,
         out_specs=vmem,
         scratch_shapes=[
+            pltpu.SMEM((2,), jnp.int32),
+            pltpu.VMEM((64, SAMPLES), F32),
+            pltpu.VMEM((1, 64), jnp.int32),
+            pltpu.VMEM((256, 256), BF16),
+            pltpu.VMEM((256, 256), BF16),
+            pltpu.VMEM((256, 256), BF16),
+            pltpu.VMEM((256, 256), BF16),
+            pltpu.VMEM((16, 128), F32),
+            pltpu.VMEM((64, 1), F32),
             pltpu.VMEM((8, 64, 256), BF16),
             pltpu.VMEM((8, 64, 256), BF16),
             pltpu.VMEM((8, 64, 256), F32),
@@ -483,7 +504,7 @@
             pltpu.VMEM((2, 4, 64, 512), F32),
             pltpu.VMEM((2, 4, 64, 512), BF16),
             pltpu.VMEM((2, 4, 64, 512), BF16),
-            dma,
+            dma((9,)),
             dma((8,)), dma((8,)),
             dma((4,)), dma((4,)),
             dma((8,)), dma((8,)),
@@ -495,10 +516,10 @@
             dma((2, 4)), dma((2, 4)),
         ],
         compiler_params=pltpu.CompilerParams(
-            collective_id=0, has_side_effects=True, vmem_limit_bytes=40 * 1024 * 1024
+            collective_id=0, has_side_effects=True, vmem_limit_bytes=56 * 1024 * 1024
         ),
         name="correlate",
-    )(plan, strain.reshape(64, SAMPLES), validity, t1h, t1l, t2h, t2l, twiddle, lag)
+    )(plan, strain, validity.T, t1h, t1l, t2h, t2l, twiddle, lag)
 
 
 def solution(mesh):

time: 93.6 us -> 81.3 us (0.87)
  local copies, waits for them, and re-layouts: 9.47 us -> 2.26 us
  Pallas kernels: 83.8 us -> 78.9 us
    unnamed x17 -> x1, local copies, waits for them, and re-layouts: 9.47 us -> 2.26 us
    pallas_call x1, Pallas kernels: 83.8 us -> 78.9 us  [shards(): pl.pallas_call(kernel, out_shape=jax.ShapeDtypeStruct((ROUNDS, 4, 64, LAG...]
where the time goes in v2:
time: 81.3 us; the launch traced here: 81.1 us
  Pallas kernels  78.9 us (97%)
  local copies, waits for them, and re-layouts  2.26 us (3%)
    pallas_call x1, Pallas kernels, shards(): pl.pallas_call(kernel, out_shape=jax.ShapeDtypeStruct((ROUNDS, 4, 64, LAG...  78.9 us
    unnamed x1, local copies, waits for them, and re-layouts  2.26 us

profile of v2, /device:TPU:1, one launch (start us, length us, event | category | flops | bytes accessed | tf_op | source)
XLA Modules:
  0.0 81.1 jit_solution(5548949782107664392)
XLA Ops:
  0.0 78.9 %correlate.1 = f32[2,4,64,401]{3,2,1,0:T(8,128)} custom-call(s32[2]{0:T(128)} %plan_in.1, f32[64,1,2048]{2,1,0:T(1,128)} %x_in.1, s32[1,64]{1,0:T(1,128)} %bitcast.1, bf16[256,256]{1,0:T(8,128)(2,1)} %constant.12.clone.t1h_in, bf16[256,256]{1,0:T(8,128)(2,1)} %constant.13.clone.t1l_in, bf16[256,256]{1,0:T(8,128)(2,1)} %constant.14.clone.t2h_in, ...), custom_call_target="tpu_custom_call" | custom-call | tf_op jit(solution)/shard_map/correlate/pallas_call | solution.py:468
  78.9 2.3 %copy.11 = f32[2,4,64,401]{3,2,1,0:T(8,128)} copy(f32[2,4,64,401]{3,2,1,0:T(8,128)} %correlate.1) | data formatting | bytes 1642496

commit v3 on v2

--- a/solution.py
+++ b/solution.py
@@ -93,9 +93,9 @@
 
 def kernel(
     plan_in, x_in, valid_in, t1h_in, t1l_in, t2h_in, t2l_in, twiddle_in, lag_in, out,
-    plan, x, flags, t1h, t1l, t2h, t2l, twiddle, valid, zh_, zl_, spec, ws, zw, wg, v, fl, fv, fpad, fto, ctab, crecv, inv,
+    plan, x, flags, obuf, t1h, t1l, t2h, t2l, twiddle, valid, zh_, zl_, spec, ws, zw, wg, v, fl, fv, fpad, fto, ctab, crecv, inv,
     a_, b_, c_, d_, xs, xr, lag, keep, zs, zr,
-    in_sems, y1s, y1r, zws, zwr, y2s, y2r, p_s, p_r, f1s, f1r, fxs, fxr, cs, cr, ys, yr, zss, zrr,
+    in_sems, out_sems, y1s, y1r, zws, zwr, y2s, y2r, p_s, p_r, f1s, f1r, fxs, fxr, cs, cr, ys, yr, zss, zrr,
 ):
     chan, seg = lax.axis_index("chan"), lax.axis_index("seg")
     core = lax.rem(chan, 2)
@@ -114,7 +114,7 @@
 
     other = (chan, 2 * y + oz)
     ahead = (chan_at(2), seg)
-    jump = (chan_at(1 + 2 * core), seg)
+    after = (chan_at(1), seg)
     mate = (chan_at(1 - 2 * core), seg)
 
     def remote(src, dst, send, recv, device):
@@ -124,23 +124,29 @@
 
     barrier = pltpu.get_barrier_semaphore()
     senders = [on_y(at_y(s)) for s in range(1, 8)] + [other]
-    senders += [(chan_at(-2), seg), (chan_at(-3 + 2 * core), seg), mate]
+    senders += [(chan_at(-1), seg), (chan_at(-2), seg), mate]
     for device in senders:
         pl.semaphore_signal(barrier, inc=1, device_id=device, device_id_type=MESH)
-    loads = [pltpu.make_async_copy(x_in.at[:, 0, :], x, in_sems.at[0])]
+    strain_loads = []
+    for g in range(4):
+        rows = pl.ds(16 * g, 16)
+        strain_loads.append(pltpu.make_async_copy(x_in.at[rows, 0, :], x.at[rows], in_sems.at[9 + g]))
+        strain_loads[-1].start()
+    loads = []
     pairs_in = [(twiddle_in, twiddle), (valid_in, flags), (t1h_in, t1h), (t1l_in, t1l), (t2h_in, t2h), (t2l_in, t2l)]
     pairs_in += [(plan_in, plan), (lag_in.at[pl.ds(4 * zh, 4)], lag)]
     for number, (src, dst) in enumerate(pairs_in):
-        loads.append(pltpu.make_async_copy(src, dst, in_sems.at[number + 1]))
+        loads.append(pltpu.make_async_copy(src, dst, in_sems.at[number]))
     for copy in loads:
         copy.start()
-    for copy in loads[:3]:
+    for copy in loads[:2]:
         copy.wait()
     square_flags = jnp.broadcast_to(flags[...].astype(F32), (64, 64))
     valid[...] = jnp.transpose(square_flags)[:, 0:1]
 
     def transform(g, carry):
         rows = pl.ds(pl.multiple_of(g * 16, 16), 16)
+        pltpu.make_async_copy(x_in.at[rows, 0, :], x.at[rows], in_sems.at[9 + g]).wait()
         ys_ = first_stage([x[rows, 128 * s : 128 * s + 128] for s in range(16)])
         pairs = [(ys_[0], ys_[8])]
         for k in range(1, 8):
@@ -156,7 +162,7 @@
 
     lax.fori_loop(0, 4, transform, 0)
 
-    for copy in loads[3:8]:
+    for copy in loads[2:7]:
         copy.wait()
 
     def product(high, low, th, tl):
@@ -206,7 +212,7 @@
 
     pl.semaphore_wait(barrier, 11)
 
-    z_sends, y1_sends, y2_sends, f_sends = [], [], [], []
+    z_sends, y1_sends, f_sends = [], [], []
     for step in range(4):
         k = lax.rem(kappa + step, 4)
         z_sends.append(remote(ws.at[4 * oz + k], zw.at[k], zws.at[k], zwr.at[k], other))
@@ -223,68 +229,97 @@
     wg[zh, :, y] = ws[4 * zh + kappa]
 
     def put_p1(half, j):
-        piece = wg.at[half, j]
-        first = remote(piece, v.at[1, half, j], p_s.at[0, half, j], p_r.at[1, half, j], ahead)
-        second = remote(
-            piece, v.at[2 * core, half, j], p_s.at[1, half, j], p_r.at[2 * core, half, j], jump
-        )
-        return first, second
+        return remote(wg.at[half, j], v.at[1, half, j], p_s.at[0, half, j], p_r.at[1, half, j], ahead)
+
+    def put_own(half, j):
+        return remote(wg.at[half, j], v.at[0, half, j], p_s.at[1, half, j], p_r.at[0, half, j], after)
+
+    def put_on(half, j):
+        return remote(v.at[1, half, j], v.at[2, half, j], p_s.at[1, half, j], p_r.at[2, half, j], after)
 
     def put_p2(half, j):
         return remote(
             v.at[1, half, j], v.at[2 - 2 * core, half, j], p_s.at[2, half, j], p_r.at[2 - 2 * core, half, j], mate
         )
 
+    def start_first(half, j):
+        put_p1(half, j).start()
+
+        @pl.when(core == 0)
+        def _():
+            put_own(half, j).start()
+
+    def start_second(half, j):
+        arrived(1, half, j)
+
+        @pl.when(core == 1)
+        def _():
+            put_on(half, j).start()
+
+        put_p2(half, j).start()
+
     def arrived(slot, half, j):
         remote(v.at[slot, half, j], v.at[slot, half, j], p_s.at[0, half, j], p_r.at[slot, half, j], ahead).wait_recv()
 
+    def put_y2(part, step):
+        k = lax.rem(kappa + step, 4)
+        rows = pl.ds(2 * part, 2)
+        return remote(
+            zw.at[k, rows], wg.at[oz, rows, y], y2s.at[part, step], y2r.at[part, step], on_y(at_y(step))
+        )
+
+    for step in range(4):
+        z_sends[step].wait_recv()
+        for far in (4, 0):
+            if step + far > 0:
+                put_y2(0, step + far).start()
+    for step in (4, 5, 1, 6, 2, 7, 3):
+        put_y2(1, step).start()
+    wg[oz, :, y] = zw[kappa]
     for copy in y1_sends:
         copy.wait_recv()
 
-    def start_p1(half):
-        def body(j, carry):
-            for copy in put_p1(half, j):
-                copy.start()
-            return carry
-
-        lax.fori_loop(0, 4, body, 0)
-
-    start_p1(zh)
-    for step in range(4):
-        k = lax.rem(kappa + step, 4)
-        z_sends[step].wait_recv()
-        for far in (4, 0):
-            if step + far == 0:
-                wg[oz, :, y] = zw[k]
-                continue
-            row = at_y(step + far)
-            y2_sends.append(
-                remote(zw.at[k], wg.at[oz, :, y], y2s.at[step + far], y2r.at[step + far], on_y(row))
-            )
-            y2_sends[-1].start()
+    def start_p1(j, carry):
+        start_first(zh, j)
+        return carry
+
+    lax.fori_loop(0, 4, start_p1, 0)
 
     for copy in f_sends:
         copy.wait_recv()
     flag_sends = [
         remote(fl, fv.at[1], fxs.at[0], fxr.at[1], ahead),
-        remote(fl, fv.at[2 * core], fxs.at[1], fxr.at[2 * core], jump),
+        remote(fl, fv.at[0], fxs.at[1], fxr.at[0], after),
     ]
-    for copy in flag_sends:
-        copy.start()
+    flag_sends[0].start()
+
+    @pl.when(core == 0)
+    def _():
+        flag_sends[1].start()
+
+    def start_direct(part):
+        for step in range(1, 8):
+            put_y2(part, step).wait_recv()
+        for j in (2 * part, 2 * part + 1):
+            start_first(oz, j)
+
+    start_direct(0)
 
     def start_p2(j, carry):
-        arrived(1, zh, j)
-        put_p2(zh, j).start()
+        start_second(zh, j)
         return carry
 
     lax.fori_loop(0, 4, start_p2, 0)
-    for copy in y2_sends:
-        copy.wait_recv()
-    start_p1(oz)
-
+    start_direct(1)
     remote(fv.at[1], fv.at[1], fxs.at[0], fxr.at[1], ahead).wait_recv()
     flag_sends.append(remote(fv.at[1], fv.at[2 - 2 * core], fxs.at[2], fxr.at[2 - 2 * core], mate))
     flag_sends[-1].start()
+
+    @pl.when(core == 1)
+    def _():
+        remote(fv.at[1], fv.at[2], fxs.at[1], fxr.at[2], after).start()
+
+    start_second(oz, 0)
 
     first_half = lane < 64
     sign = jnp.where(first_half, 1.0, -1.0).astype(F32)
@@ -361,23 +396,36 @@
     def lag_stage(r, j):
         for t in range(3):
             put_cross(r, j, t).wait_recv()
-        zs[r, j] = lagged(r, j, oz).astype(BF16)
+        theirs = lagged(r, j, oz)
+        for t in range(3):
+            zs[r, j, 64 * t : 64 * t + 64, :] = theirs[:, 128 * t : 128 * t + 128].astype(BF16)
+        tail = theirs[0:16, 384:512]
+        for i in range(1, 4):
+            tail += pltpu.roll(theirs[16 * i : 16 * i + 16, 384:512], 32 * i, 1)
+        zs[r, j, 192:208, :] = tail.astype(BF16)
         put_lags(r, j).start()
         keep[r, j] = lagged(r, j, zh)
 
+    def put_out(r, j):
+        rows = pl.ds(pl.multiple_of(16 * j, 16), 16)
+        return pltpu.make_async_copy(obuf.at[r, :, rows, :], out.at[r, :, rows, :], out_sems.at[r, j])
+
     def finish(r, j):
         put_lags(r, j).wait_recv()
-        total = keep[r, j] + zr[r, j].astype(F32)
         rows = pl.ds(pl.multiple_of(16 * j, 16), 16)
+        tail = zr[r, j, 192:208, :].astype(F32)
         for i in range(4):
-            scale = inv[r, i, rows, 0:1]
-            out[r, i, rows, :] = (total[16 * i : 16 * i + 16, :] * scale)[:, :LAGS]
-
-    def start_round(j):
-        arrived(1, oz, j)
-        put_p2(oz, j).start()
-
-    start_round(0)
+            scale = inv[r, i, rows, :]
+            for t in range(3):
+                theirs = zr[r, j, 64 * t + 16 * i : 64 * t + 16 * i + 16, :].astype(F32)
+                mine = keep[r, j, 16 * i : 16 * i + 16, 128 * t : 128 * t + 128]
+                obuf[r, i, rows, 128 * t : 128 * t + 128] = (mine + theirs) * scale
+            theirs = pltpu.roll(tail, 128 - 32 * i, 1) if i else tail
+            mine = keep[r, j, 16 * i : 16 * i + 16, 384:512]
+            obuf[r, i, rows, 384:LAGS] = ((mine + theirs) * scale)[:, : LAGS - 384]
+        put_out(r, j).start()
+
+    start_second(oz, 1)
 
     wide = lax.broadcasted_iota(jnp.int32, (64, 128), 1)
     fpad[...] = jnp.zeros((128, 128), F32)
@@ -398,18 +446,18 @@
     count_send = remote(ctab, crecv, cs, cr, other)
     count_send.start()
 
-    loads[8].wait()
+    loads[7].wait()
 
     def main_loop(j, carry):
         arrived(0, zh, j)
+        arrived(2, zh, j)
         arrived(0, oz, j)
-        arrived(2, zh, j)
         arrived(2, oz, j)
         cross_all(0, j)
 
-        @pl.when(j < 3)
+        @pl.when(j < 2)
         def _():
-            start_round(j + 1)
+            start_second(oz, j + 2)
 
         cross_all(1, j)
 
@@ -443,37 +491,41 @@
         for r in range(ROUNDS):
             finish(r, j)
 
-    for copy in z_sends + y1_sends + y2_sends + f_sends + flag_sends + [count_send]:
+    for copy in z_sends + y1_sends + f_sends + flag_sends + [count_send]:
         copy.wait_send()
 
     def drain(j, carry):
         for half in range(2):
-            for copy in put_p1(half, j):
-                copy.wait_send()
+            put_p1(half, j).wait_send()
+            put_own(half, j).wait_send()
             put_p2(half, j).wait_send()
         for r in range(ROUNDS):
             for t in range(3):
                 put_cross(r, j, t).wait_send()
             put_lags(r, j).wait_send()
+            put_out(r, j).wait()
         return carry
 
     lax.fori_loop(0, 4, drain, 0)
+    for part in range(2):
+        for step in range(1, 8):
+            put_y2(part, step).wait_send()
 
 
 def shards(strain, validity, plan):
     t1h, t1l, t2h, t2l, twiddle = (jnp.asarray(t) for t in dft_tables())
     lag = jnp.asarray(lag_table())
-    vmem = pl.BlockSpec(memory_space=pltpu.VMEM)
     dma = pltpu.SemaphoreType.DMA
     return pl.pallas_call(
         kernel,
         out_shape=jax.ShapeDtypeStruct((ROUNDS, 4, 64, LAGS), F32),
         in_specs=[pl.BlockSpec(memory_space=pltpu.HBM)] * 9,
-        out_specs=vmem,
+        out_specs=pl.BlockSpec(memory_space=pltpu.HBM),
         scratch_shapes=[
             pltpu.SMEM((2,), jnp.int32),
             pltpu.VMEM((64, SAMPLES), F32),
             pltpu.VMEM((1, 64), jnp.int32),
+            pltpu.VMEM((2, 4, 64, LAGS), F32),
             pltpu.VMEM((256, 256), BF16),
             pltpu.VMEM((256, 256), BF16),
             pltpu.VMEM((256, 256), BF16),
@@ -502,12 +554,12 @@
             pltpu.VMEM((2, 4, 4, 128, 256), BF16),
             pltpu.VMEM((4, 256, 512), BF16),
             pltpu.VMEM((2, 4, 64, 512), F32),
-            pltpu.VMEM((2, 4, 64, 512), BF16),
-            pltpu.VMEM((2, 4, 64, 512), BF16),
-            dma((9,)),
+            pltpu.VMEM((2, 4, 208, 128), BF16),
+            pltpu.VMEM((2, 4, 208, 128), BF16),
+            dma((13,)), dma((2, 4)),
             dma((8,)), dma((8,)),
             dma((4,)), dma((4,)),
-            dma((8,)), dma((8,)),
+            dma((2, 8)), dma((2, 8)),
             dma((3, 2, 4)), dma((3, 2, 4)),
             dma((8,)), dma((8,)),
             dma((3,)), dma((3,)),

time: 81.3 us -> 76.5 us (0.941)
  the two profiles are of different devices: /device:TPU:1 before, /device:TPU:8 now
where the time goes in v3:
time: 76.5 us; the launch traced here: 76.3 us
  Pallas kernels  74 us (97%)
  local copies, waits for them, and re-layouts  2.26 us (3%)
    pallas_call x1, Pallas kernels, shards(): pl.pallas_call(kernel, out_shape=jax.ShapeDtypeStruct((ROUNDS, 4, 64, LAG...  74 us
    unnamed x1, local copies, waits for them, and re-layouts  2.26 us

profile of v3, /device:TPU:8, one launch (start us, length us, event | category | flops | bytes accessed | tf_op | source)
XLA Modules:
  0.0 76.3 jit_solution(11858856702735749931)
XLA Ops:
  0.0 74.0 %correlate.1 = f32[2,4,64,401]{3,2,1,0:T(8,128)} custom-call(s32[2]{0:T(128)} %plan_in.1, f32[64,1,2048]{2,1,0:T(1,128)} %x_in.1, s32[1,64]{1,0:T(1,128)} %bitcast.1, bf16[256,256]{1,0:T(8,128)(2,1)} %constant.12.clone.t1h_in, bf16[256,256]{1,0:T(8,128)(2,1)} %constant.13.clone.t1l_in, bf16[256,256]{1,0:T(8,128)(2,1)} %constant.14.clone.t2h_in, ...), custom_call_target="tpu_custom_call" | custom-call | tf_op jit(solution)/shard_map/correlate/pallas_call | solution.py:519
  74.0 2.3 %copy.11 = f32[2,4,64,401]{3,2,1,0:T(8,128)} copy(f32[2,4,64,401]{3,2,1,0:T(8,128)} %correlate.1) | data formatting | bytes 1642496

commit v4 on v3

--- a/solution.py
+++ b/solution.py
@@ -213,9 +213,11 @@
     pl.semaphore_wait(barrier, 11)
 
     z_sends, y1_sends, f_sends = [], [], []
-    for step in range(4):
-        k = lax.rem(kappa + step, 4)
-        z_sends.append(remote(ws.at[4 * oz + k], zw.at[k], zws.at[k], zwr.at[k], other))
+    for part in range(2):
+        rows = pl.ds(2 * part, 2)
+        z_sends.append(
+            remote(ws.at[pl.ds(4 * oz, 4), rows], zw.at[:, rows], zws.at[part], zwr.at[part], other)
+        )
         z_sends[-1].start()
     for step in (4, 3, 5, 2, 6, 1, 7):
         row = at_y(step)
@@ -268,22 +270,16 @@
             zw.at[k, rows], wg.at[oz, rows, y], y2s.at[part, step], y2r.at[part, step], on_y(at_y(step))
         )
 
-    for step in range(4):
-        z_sends[step].wait_recv()
-        for far in (4, 0):
-            if step + far > 0:
-                put_y2(0, step + far).start()
-    for step in (4, 5, 1, 6, 2, 7, 3):
-        put_y2(1, step).start()
+    for part in range(2):
+        z_sends[part].wait_recv()
+        for step in (4, 3, 5, 2, 6, 1, 7):
+            put_y2(part, step).start()
     wg[oz, :, y] = zw[kappa]
     for copy in y1_sends:
         copy.wait_recv()
 
-    def start_p1(j, carry):
-        start_first(zh, j)
-        return carry
-
-    lax.fori_loop(0, 4, start_p1, 0)
+    start_first(zh, 0)
+    start_first(zh, 1)
 
     for copy in f_sends:
         copy.wait_recv()
@@ -302,14 +298,12 @@
             put_y2(part, step).wait_recv()
         for j in (2 * part, 2 * part + 1):
             start_first(oz, j)
-
+            if part == 0:
+                start_first(zh, j + 2)
+
+    start_second(zh, 0)
+    start_second(zh, 1)
     start_direct(0)
-
-    def start_p2(j, carry):
-        start_second(zh, j)
-        return carry
-
-    lax.fori_loop(0, 4, start_p2, 0)
     start_direct(1)
     remote(fv.at[1], fv.at[1], fxs.at[0], fxr.at[1], ahead).wait_recv()
     flag_sends.append(remote(fv.at[1], fv.at[2 - 2 * core], fxs.at[2], fxr.at[2 - 2 * core], mate))
@@ -404,6 +398,8 @@
             tail += pltpu.roll(theirs[16 * i : 16 * i + 16, 384:512], 32 * i, 1)
         zs[r, j, 192:208, :] = tail.astype(BF16)
         put_lags(r, j).start()
+
+    def keep_stage(r, j):
         keep[r, j] = lagged(r, j, zh)
 
     def put_out(r, j):
@@ -428,23 +424,25 @@
     start_second(oz, 1)
 
     wide = lax.broadcasted_iota(jnp.int32, (64, 128), 1)
-    fpad[...] = jnp.zeros((128, 128), F32)
-    for s in range(8):
-        fpad[s : s + 1, :] = fl[s]
-    fto[...] = jnp.transpose(fpad[...])
-    remote(fv.at[0], fv.at[0], fxs.at[0], fxr.at[0], ahead).wait_recv()
-    remote(fv.at[2], fv.at[2], fxs.at[0], fxr.at[2], ahead).wait_recv()
-    table = jnp.zeros((64, 128), F32)
-    for r in range(ROUNDS):
+    count_send = remote(ctab, crecv, cs, cr, other)
+
+    def counting():
+        fpad[...] = jnp.zeros((128, 128), F32)
         for s in range(8):
-            fpad[s : s + 1, :] = chosen(r, [fv[d, s] for d in range(3)])
-        partner = jnp.transpose(fpad[...])[0:64, :]
-        for i in range(8):
-            number = jnp.sum(partner * fto[pl.ds(8 * y + i, 1), :], axis=1, keepdims=True)
-            table = jnp.where(wide == 8 * r + i, number, table)
-    ctab[...] = table
-    count_send = remote(ctab, crecv, cs, cr, other)
-    count_send.start()
+            fpad[s : s + 1, :] = fl[s]
+        fto[...] = jnp.transpose(fpad[...])
+        remote(fv.at[0], fv.at[0], fxs.at[0], fxr.at[0], ahead).wait_recv()
+        remote(fv.at[2], fv.at[2], fxs.at[0], fxr.at[2], ahead).wait_recv()
+        table = jnp.zeros((64, 128), F32)
+        for r in range(ROUNDS):
+            for s in range(8):
+                fpad[s : s + 1, :] = chosen(r, [fv[d, s] for d in range(3)])
+            partner = jnp.transpose(fpad[...])[0:64, :]
+            for i in range(8):
+                number = jnp.sum(partner * fto[pl.ds(8 * y + i, 1), :], axis=1, keepdims=True)
+                table = jnp.where(wide == 8 * r + i, number, table)
+        ctab[...] = table
+        count_send.start()
 
     loads[7].wait()
 
@@ -453,6 +451,11 @@
         arrived(2, zh, j)
         arrived(0, oz, j)
         arrived(2, oz, j)
+
+        @pl.when(j < 2)
+        def _():
+            start_second(zh, j + 2)
+
         cross_all(0, j)
 
         @pl.when(j < 2)
@@ -461,7 +464,11 @@
 
         cross_all(1, j)
 
-        @pl.when(j == 1)
+        @pl.when(j == 0)
+        def _():
+            counting()
+
+        @pl.when(j == 2)
         def _():
             count_send.wait_recv()
             both = ctab[...] + crecv[...]
@@ -476,6 +483,8 @@
         def _():
             for r in range(ROUNDS):
                 lag_stage(r, j - 1)
+            for r in range(ROUNDS):
+                keep_stage(r, j - 1)
 
         @pl.when(j >= 2)
         def _():
@@ -487,9 +496,12 @@
     lax.fori_loop(0, 4, main_loop, 0)
     for r in range(ROUNDS):
         lag_stage(r, 3)
-    for j in (2, 3):
-        for r in range(ROUNDS):
-            finish(r, j)
+    for r in range(ROUNDS):
+        finish(r, 2)
+    for r in range(ROUNDS):
+        keep_stage(r, 3)
+    for r in range(ROUNDS):
+        finish(r, 3)
 
     for copy in z_sends + y1_sends + f_sends + flag_sends + [count_send]:
         copy.wait_send()
@@ -558,7 +570,7 @@
             pltpu.VMEM((2, 4, 208, 128), BF16),
             dma((13,)), dma((2, 4)),
             dma((8,)), dma((8,)),
-            dma((4,)), dma((4,)),
+            dma((2,)), dma((2,)),
             dma((2, 8)), dma((2, 8)),
             dma((3, 2, 4)), dma((3, 2, 4)),
             dma((8,)), dma((8,)),

time: 76.5 us -> 74.6 us (0.975)
  the two profiles are of different devices: /device:TPU:8 before, /device:TPU:2 now
where the time goes in v4:
time: 74.6 us; the launch traced here: 74.4 us
  Pallas kernels  72.1 us (97%)
  local copies, waits for them, and re-layouts  2.26 us (3%)
    pallas_call x1, Pallas kernels, shards(): pl.pallas_call(kernel, out_shape=jax.ShapeDtypeStruct((ROUNDS, 4, 64, LAG...  72.1 us
    unnamed x1, local copies, waits for them, and re-layouts  2.26 us

profile of v4, /device:TPU:2, one launch (start us, length us, event | category | flops | bytes accessed | tf_op | source)
XLA Modules:
  0.0 74.4 jit_solution(12882030373598894682)
XLA Ops:
  0.0 72.1 %correlate.1 = f32[2,4,64,401]{3,2,1,0:T(8,128)} custom-call(s32[2]{0:T(128)} %plan_in.1, f32[64,1,2048]{2,1,0:T(1,128)} %x_in.1, s32[1,64]{1,0:T(1,128)} %bitcast.1, bf16[256,256]{1,0:T(8,128)(2,1)} %constant.12.clone.t1h_in, bf16[256,256]{1,0:T(8,128)(2,1)} %constant.13.clone.t1l_in, bf16[256,256]{1,0:T(8,128)(2,1)} %constant.14.clone.t2h_in, ...), custom_call_target="tpu_custom_call" | custom-call | tf_op jit(solution)/shard_map/correlate/pallas_call | solution.py:531
  72.2 2.3 %copy.11 = f32[2,4,64,401]{3,2,1,0:T(8,128)} copy(f32[2,4,64,401]{3,2,1,0:T(8,128)} %correlate.1) | data formatting | bytes 1642496

commit v5 on v4

--- a/solution.py
+++ b/solution.py
@@ -365,16 +365,21 @@
             for i in range(8):
                 target[16 * i : 16 * i + 16, 128 * h : 128 * h + 128] = totals[i].astype(BF16)
 
-    def put_cross(r, j, t):
+    def put_cross(r, j, t, part):
+        rows = pl.ds(pl.multiple_of(64 * (zh if part else oz), 64), 64)
         return remote(
-            xs.at[r, j, t], xr.at[r, j, kappa], ys.at[r, j, t], yr.at[r, j, t], on_y(at_y(hops[t]))
+            xs.at[r, j, t, rows],
+            xr.at[r, j, kappa, rows],
+            ys.at[r, j, t, part],
+            yr.at[r, j, t, part],
+            on_y(at_y(hops[t])),
         )
 
     def cross_all(r, j):
         prepare(r, j)
         for t in range(3):
             cross(r, j, t, xs.at[r, j, t])
-            put_cross(r, j, t).start()
+            put_cross(r, j, t, 0).start()
         cross(r, j, 3, xr.at[r, j, kappa])
 
     def put_lags(r, j):
@@ -389,7 +394,7 @@
 
     def lag_stage(r, j):
         for t in range(3):
-            put_cross(r, j, t).wait_recv()
+            put_cross(r, j, t, 0).wait_recv()
         theirs = lagged(r, j, oz)
         for t in range(3):
             zs[r, j, 64 * t : 64 * t + 64, :] = theirs[:, 128 * t : 128 * t + 128].astype(BF16)
@@ -400,6 +405,8 @@
         put_lags(r, j).start()
 
     def keep_stage(r, j):
+        for t in range(3):
+            put_cross(r, j, t, 1).wait_recv()
         keep[r, j] = lagged(r, j, zh)
 
     def put_out(r, j):
@@ -462,7 +469,14 @@
         def _():
             start_second(oz, j + 2)
 
+        @pl.when(j >= 1)
+        def _():
+            lag_stage(0, j - 1)
+
         cross_all(1, j)
+        for r in range(ROUNDS):
+            for t in range(3):
+                put_cross(r, j, t, 1).start()
 
         @pl.when(j == 0)
         def _():
@@ -481,14 +495,12 @@
 
         @pl.when(j >= 1)
         def _():
+            lag_stage(1, j - 1)
+
+        @pl.when(j >= 2)
+        def _():
             for r in range(ROUNDS):
-                lag_stage(r, j - 1)
-            for r in range(ROUNDS):
-                keep_stage(r, j - 1)
-
-        @pl.when(j >= 2)
-        def _():
-            for r in range(ROUNDS):
+                keep_stage(r, j - 2)
                 finish(r, j - 2)
 
         return carry
@@ -497,6 +509,7 @@
     for r in range(ROUNDS):
         lag_stage(r, 3)
     for r in range(ROUNDS):
+        keep_stage(r, 2)
         finish(r, 2)
     for r in range(ROUNDS):
         keep_stage(r, 3)
@@ -513,7 +526,8 @@
             put_p2(half, j).wait_send()
         for r in range(ROUNDS):
             for t in range(3):
-                put_cross(r, j, t).wait_send()
+                for part in range(2):
+                    put_cross(r, j, t, part).wait_send()
             put_lags(r, j).wait_send()
             put_out(r, j).wait()
         return carry
@@ -576,7 +590,7 @@
             dma((8,)), dma((8,)),
             dma((3,)), dma((3,)),
             dma, dma,
-            dma((2, 4, 3)), dma((2, 4, 3)),
+            dma((2, 4, 3, 2)), dma((2, 4, 3, 2)),
             dma((2, 4)), dma((2, 4)),
         ],
         compiler_params=pltpu.CompilerParams(

time: 74.6 us -> 72.6 us (0.973)
  the two profiles are of different devices: /device:TPU:2 before, /device:TPU:1 now
where the time goes in v5:
time: 72.6 us; the launch traced here: 72.2 us
  Pallas kernels  70 us (96%)
  local copies, waits for them, and re-layouts  2.26 us (3%)
    pallas_call x1, Pallas kernels, shards(): pl.pallas_call(kernel, out_shape=jax.ShapeDtypeStruct((ROUNDS, 4, 64, LAG...  70 us
    unnamed x1, local copies, waits for them, and re-layouts  2.26 us

profile of v5, /device:TPU:1, one launch (start us, length us, event | category | flops | bytes accessed | tf_op | source)
XLA Modules:
  0.0 72.2 jit_solution(712359995951181263)
XLA Ops:
  0.0 70.0 %correlate.1 = f32[2,4,64,401]{3,2,1,0:T(8,128)} custom-call(s32[2]{0:T(128)} %plan_in.1, f32[64,1,2048]{2,1,0:T(1,128)} %x_in.1, s32[1,64]{1,0:T(1,128)} %bitcast.1, bf16[256,256]{1,0:T(8,128)(2,1)} %constant.12.clone.t1h_in, bf16[256,256]{1,0:T(8,128)(2,1)} %constant.13.clone.t1l_in, bf16[256,256]{1,0:T(8,128)(2,1)} %constant.14.clone.t2h_in, ...), custom_call_target="tpu_custom_call" | custom-call | tf_op jit(solution)/shard_map/correlate/pallas_call | solution.py:545
  70.0 2.3 %copy.11 = f32[2,4,64,401]{3,2,1,0:T(8,128)} copy(f32[2,4,64,401]{3,2,1,0:T(8,128)} %correlate.1) | data formatting | bytes 1642496

commit v6 on v5

--- a/solution.py
+++ b/solution.py
@@ -472,6 +472,7 @@
         @pl.when(j >= 1)
         def _():
             lag_stage(0, j - 1)
+            lag_stage(1, j - 1)
 
         cross_all(1, j)
         for r in range(ROUNDS):
@@ -492,10 +493,6 @@
                         jnp.where(wide == 8 * r + 4 * zh + i, both, 0.0), axis=1, keepdims=True
                     )
                     inv[r, i] = jnp.broadcast_to(1.0 / jnp.maximum(number, 1.0), (64, 128))
-
-        @pl.when(j >= 1)
-        def _():
-            lag_stage(1, j - 1)
 
         @pl.when(j >= 2)
         def _():

time: 72.6 us -> 73.3 us (level)
  the two profiles are of different devices: /device:TPU:1 before, /device:TPU:16 now
where the time goes in v6:
time: 73.3 us; the launch traced here: 73.1 us
  Pallas kernels  70.9 us (97%)
  local copies, waits for them, and re-layouts  2.26 us (3%)
    pallas_call x1, Pallas kernels, shards(): pl.pallas_call(kernel, out_shape=jax.ShapeDtypeStruct((ROUNDS, 4, 64, LAG...  70.9 us
    unnamed x1, local copies, waits for them, and re-layouts  2.26 us

profile of v6, /device:TPU:16, one launch (start us, length us, event | category | flops | bytes accessed | tf_op | source)
XLA Modules:
  0.0 73.1 jit_solution(16822668799410365480)
XLA Ops:
  0.0 70.9 %correlate.1 = f32[2,4,64,401]{3,2,1,0:T(8,128)} custom-call(s32[2]{0:T(128)} %plan_in.1, f32[64,1,2048]{2,1,0:T(1,128)} %x_in.1, s32[1,64]{1,0:T(1,128)} %bitcast.1, bf16[256,256]{1,0:T(8,128)(2,1)} %constant.12.clone.t1h_in, bf16[256,256]{1,0:T(8,128)(2,1)} %constant.13.clone.t1l_in, bf16[256,256]{1,0:T(8,128)(2,1)} %constant.14.clone.t2h_in, ...), custom_call_target="tpu_custom_call" | custom-call | tf_op jit(solution)/shard_map/correlate/pallas_call | solution.py:542
  70.9 2.3 %copy.11 = f32[2,4,64,401]{3,2,1,0:T(8,128)} copy(f32[2,4,64,401]{3,2,1,0:T(8,128)} %correlate.1) | data formatting | bytes 1642496
